TPU v7x, 32 devices: a whole 2x2x4 slice. The times are simulated.
32 devices in a mesh: runs: 2 (over x), tm: 8 (over z, y), hyd: 2 (over core).
Axes of the slice: x: 2, y: 2, z: 4, core: 2. Of those that a mesh axis runs over, the one named last changes fastest.
Arguments:
- record: bfloat16 [524160, 1024], P(('runs', 'tm'), 'hyd'), parts along dimension 0, may hold values from -6 to 6
- chips: int32 [4095], replicated, may hold values from -1 to 1, as said below
- steer_lags: int32 [1024, 256], P('hyd'), may hold values from 0 to 7
Outputs:
- power: float32 [128, 512, 256], P('runs', 'tm', 'hyd'), parts along dimension 0
There are 2 independent parts, one for each index of `runs`. A program takes and returns all parts, laid end to end along the dimension named above; an argument that names none is the same for every part. Nothing has to cross between parts.
Inputs may be any that keep to these rules, and one draw needn't show every extreme that they name: The chips are +1 or -1 and form one period of a maximal-length sequence of period 4095, starting at a drawn phase.
All inputs are finite; a program needn't handle non-finite values.
Results may differ from a plain program's by a relative error of at most 0.0047.
Values may be sent and summed in bfloat16 or wider, within the bound.
A program may use at most 256 MiB of HBM per device.

v0:
```python
import math

import jax
import jax.numpy as jnp
from jax import lax
from jax.sharding import PartitionSpec as P

CODE = 4095
HYDRO = 1024
DELAYS = 512
PERIODS = 64
BEAMS = 256
MAXLAG = 8


def passed_along(array, axis, by):
    length = lax.axis_size(axis)
    pairs = [(i, i + by) for i in range(length) if 0 <= i + by < length]
    return lax.ppermute(array, axis, pairs)


def toeplitz_code(chips):
    seg_len = CODE + DELAYS - 1
    padded = jnp.concatenate([chips.astype(jnp.float32), jnp.zeros((DELAYS,), jnp.float32)])
    tiled = jnp.tile(padded, DELAYS)[: DELAYS * seg_len]
    return tiled.reshape(DELAYS, seg_len).astype(jnp.bfloat16)


def dft_table(length):
    freq = jnp.arange(length, dtype=jnp.int32)
    phase = (freq[:, None] * freq[None, :] % length).astype(jnp.float32) * (2.0 * math.pi / length)
    weight = 1.0 / math.sqrt(length)
    return jnp.concatenate([jnp.cos(phase) * weight, -jnp.sin(phase) * weight], 0).astype(
        jnp.bfloat16
    )


def body(record, chips, steer_lags):
    hyd_local = record.shape[1]
    tm_size = lax.axis_size("tm")
    local_periods = PERIODS // tm_size
    delay_rows = DELAYS // tm_size
    seg_len = CODE + DELAYS - 1
    norm_code = 1.0 / math.sqrt(CODE)
    tail_rows = passed_along(record[: DELAYS - 1], "tm", -1)
    extended = jnp.concatenate([record, tail_rows], 0)
    toeplitz = toeplitz_code(chips)
    profile_list = []
    for period in range(local_periods):
        segment = extended[period * CODE : period * CODE + seg_len]
        profile_list.append(
            (jnp.dot(toeplitz, segment, preferred_element_type=jnp.float32) * norm_code).astype(
                jnp.bfloat16
            )
        )
    profiles = jnp.stack(profile_list, 0)
    transform = dft_table(PERIODS)
    received = lax.all_to_all(profiles, "tm", split_axis=1, concat_axis=0, tiled=True)
    trailing = received.shape[1:]
    flattened = received.reshape(received.shape[0], -1)
    spectral = jnp.dot(transform, flattened, preferred_element_type=jnp.float32).astype(
        jnp.bfloat16
    )
    spectrum = spectral.reshape((2, received.shape[0]) + trailing)
    next_rows = passed_along(spectrum[:, :, : MAXLAG - 1, :], "tm", -1)
    spec_ext = jnp.concatenate([spectrum, next_rows], 2)
    norm_hydro = 1.0 / math.sqrt(HYDRO)
    shifted_list = [
        spec_ext[:, :, offset : offset + delay_rows, :].reshape(2 * PERIODS * delay_rows, hyd_local)
        for offset in range(MAXLAG)
    ]
    beam_local = BEAMS // lax.axis_size("hyd")
    partial_sum = jnp.zeros((2 * PERIODS * delay_rows, BEAMS), jnp.float32)
    for offset in range(MAXLAG):
        selector = (steer_lags == offset).astype(jnp.bfloat16)
        partial_sum = partial_sum + jnp.dot(
            shifted_list[offset], selector, preferred_element_type=jnp.float32
        )
    summed = lax.psum(partial_sum * norm_hydro, "hyd")
    owned = lax.dynamic_slice_in_dim(summed, lax.axis_index("hyd") * beam_local, beam_local, 1)
    owned = owned.reshape(2, PERIODS, delay_rows, beam_local)
    return owned[0] * owned[0] + owned[1] * owned[1]


def solution(mesh):
    in_specs = (P(("runs", "tm"), "hyd"), P(), P("hyd", None))
    out_specs = P("runs", "tm", "hyd")
    return jax.shard_map(body, mesh=mesh, in_specs=in_specs, out_specs=out_specs, check_vma=False)
```

profile of v0, /device:TPU:0, one launch (start us, length us, event | category | flops | bytes accessed | tf_op | source)
XLA Modules:
  0.0 408.4 jit_solution(9783359401931948476)
XLA Ops:
  9.6 2.5 tile.10
  12.1 11.8 %tile.11 = bf16[2358784]{0:T(1024)(128)(2,1)} reshape(bf16[512,4607]{1,0:T(8,128)(2,1)} %tile.10) | data formatting | bytes 9435136 | tf_op jit(solution)/shard_map/tile | solution.py:25
  23.9 5.7 %slice.85 = bf16[2358272]{0:T(1024)(128)(2,1)} slice(bf16[2358784]{0:T(1024)(128)(2,1)} %tile.11), slice={[0:2358272]} | slice | bytes 9433088 | tf_op jit(solution)/shard_map/slice | solution.py:25
  29.6 11.3 %convert_element_type.50 = bf16[512,4606]{1,0:T(8,128)(2,1)} reshape(bf16[2358272]{0:T(1024)(128)(2,1)} %slice.85) | data formatting | bytes 9433088 | tf_op jit(solution)/shard_map/convert_element_type | solution.py:26
  41.0 7.3 %fusion.65 = bf16[8,512,512]{2,1,0:T(8,128)(2,1)} fusion(bf16[512,4606]{1,0:T(8,128)(2,1)} %convert_element_type.50, bf16[32760,512]{1,0:T(8,128)(2,1)} %param.3), kind=kOutput, calls=%fused_computation.47 | convolution fusion | flops 2415394816 | bytes 9961472 | tf_op jit(solution)/shard_map/dot_general | solution.py:52
  48.3 5.9 %fusion.73 = bf16[8,512,512]{2,1,0:T(8,128)(2,1)} fusion(bf16[8,512,512]{2,1,0:T(8,128)(2,1)} %fusion.65, bf16[512,4606]{1,0:T(8,128)(2,1)S(1)} %copy-done.1, bf16[32760,512]{1,0:T(8,128)(2,1)} %param.3), kind=kOutput, calls=%fused_computation.51 | convolution fusion | flops 2415394816 | bytes 9959424 | tf_op jit(solution)/shard_map/dot_general | solution.py:52
  54.3 6.6 %fusion.79 = bf16[8,512,512]{2,1,0:T(8,128)(2,1)} fusion(bf16[8,512,512]{2,1,0:T(8,128)(2,1)} %fusion.73, bf16[512,4606]{1,0:T(8,128)(2,1)S(1)} %copy-done.1, bf16[32760,512]{1,0:T(8,128)(2,1)} %param.3), kind=kOutput, calls=%fused_computation.53 | convolution fusion | flops 2415394816 | bytes 9959424 | tf_op jit(solution)/shard_map/dot_general | solution.py:52
  62.3 3.9 fusion.85
  66.2 3.5 fusion.91
  69.7 3.5 fusion.97
  73.2 3.5 fusion.103
  76.8 5.9 %fusion.69 = bf16[8,512,512]{2,1,0:T(8,128)(2,1)} fusion(bf16[8,512,512]{2,1,0:T(8,128)(2,1)} %fusion.103, bf16[512,4606]{1,0:T(8,128)(2,1)} %convert_element_type.50, bf16[511,512]{1,0:T(8,128)(2,1)S(1)} %collective-permute-done, bf16[32760,512]{1,0:T(8,128)(2,1)S(1)} %bitcast.82), kind=kOutput, calls=%fused_computation.49 | convolution fusion | flops 2424827904 | bytes 39312384 | tf_op jit(solution)/shard_map/dot_general | solution.py:52
  82.7 6.6 %copy.5 = bf16[8,512,512]{2,0,1:T(8,128)(2,1)} copy(bf16[8,512,512]{2,1,0:T(8,128)(2,1)} %fusion.69) | data formatting | bytes 8388608 | tf_op jit(solution)/shard_map/stack | solution.py:56
  89.3 8.4 %all-to-all-start = ((bf16[8,512,512]{2,0,1:T(8,128)(2,1)}), bf16[8,512,512]{2,0,1:T(8,128)(2,1)}, u32[]{:S(2)}, u32[]{:S(2)}) async-start(bf16[8,512,512]{2,0,1:T(8,128)(2,1)} %copy.5), calls=%async_computation | async-start | bytes 8388608 | tf_op jit(solution)/shard_map/all_to_all | solution.py:58
  98.0 92.8 %all-to-all-done = bf16[8,512,512]{2,0,1:T(8,128)(2,1)} async-done(((bf16[8,512,512]{2,0,1:T(8,128)(2,1)}), bf16[8,512,512]{2,0,1:T(8,128)(2,1)}, u32[]{:S(2)}, u32[]{:S(2)}) %all-to-all-start) | async-done | bytes 4194336 | tf_op jit(solution)/shard_map/all_to_all | solution.py:58
  190.8 3.8 copy.14
  194.6 2.6 copy.10
  197.1 5.6 %convolution_convert_fusion = bf16[128,32768]{1,0:T(8,128)(2,1)} fusion(bf16[64,32768]{1,0:T(8,128)(2,1)S(1)} %bitcast.83, bf16[64,64]{1,0:T(8,128)(2,1)S(1)} %get-tuple-element.12, bf16[64,64]{1,0:T(8,128)(2,1)S(1)} %get-tuple-element.13), kind=kOutput, calls=%fused_computation | convolution fusion | flops 541097984 | bytes 12599296 | tf_op jit(solution)/shard_map/dot_general | solution.py:61
  202.7 13.6 %reshape_reshape.3 = bf16[8192,512]{1,0:T(8,128)(2,1)} reshape(bf16[128,32768]{1,0:T(8,128)(2,1)} %convolution_convert_fusion) | data formatting | bytes 16777216 | tf_op jit(solution)/shard_map/reshape;reshape | solution.py:69
  216.4 10.2 %copy.11 = bf16[16,8,64,512]{3,2,1,0:T(8,128)(2,1)} copy(bf16[16,8,64,512]{3,1,2,0:T(8,128)(2,1)} %bitcast.69) | data formatting | bytes 16777216
  226.6 8.0 %constant_dynamic-update-slice_fusion = bf16[2,64,71,512]{3,2,1,0:T(8,128)(2,1)} fusion(bf16[2,64,64,512]{3,2,1,0:T(8,128)(2,1)} %bitcast.79), kind=kLoop, calls=%fused_computation.94 | loop fusion | bytes 16777216
  237.6 9.1 %fusion.113 = f32[8192,256]{1,0:T(8,128)} fusion(bf16[8192,512]{1,0:T(8,128)(2,1)} %reshape_reshape.3, s32[512,256]{1,0:T(8,128)S(1)} %copy-done), kind=kOutput, calls=%fused_computation.70 | convolution fusion | flops 2147614720 | bytes 17301504 | tf_op jit(solution)/shard_map/dot_general | solution.py:76
  246.7 12.5 %collective-permute-done.1 = bf16[2,64,7,512]{3,1,2,0:T(8,128)(2,1)S(1)} collective-permute-done((bf16[2,64,7,512]{3,1,2,0:T(8,128)(2,1)S(1)}, bf16[2,64,7,512]{3,1,2,0:T(8,128)(2,1)S(1)}, u32[]{:S(2)}, u32[]{:S(2)}) %collective-permute-start.1) | collective-permute-done | bytes 917536 | tf_op jit(solution)/shard_map/ppermute | solution.py:19
  260.8 52.9 %fusion.142 = (bf16[2,64,64,512]{3,2,1,0:T(8,128)(2,1)}, bf16[2,64,64,512]{3,2,1,0:T(8,128)(2,1)}, bf16[2,64,64,512]{3,2,1,0:T(8,128)(2,1)}, bf16[2,64,64,512]{3...) fusion(bf16[2,64,71,512]{3,2,1,0:T(8,128)(2,1)} %copy_dynamic-u, ...), kind=kLoop, calls=%fused_computation.106 | loop fusion | bytes 117440512 | tf_op jit(solution)/shard_map/slice | solution.py:69
  313.7 8.4 %convolution_add_fusion.6 = f32[8192,256]{1,0:T(8,128)S(1)} fusion(f32[8192,256]{1,0:T(8,128)} %fusion.113, bf16[8192,512]{1,0:T(8,128)(2,1)} %bitcast.78, s32[512,256]{1,0:T(8,128)S(1)} %copy-done), kind=kOutput, calls=%fused_computation.8 | convolution fusion | flops 2149711872 | bytes 25690112 | tf_op jit(solution)/shard_map/dot_general | solution.py:76
  322.1 6.1 %convolution_add_fusion.5 = f32[8192,256]{1,0:T(8,128)S(1)} fusion(f32[8192,256]{1,0:T(8,128)S(1)} %convolution_add_fusion.6, bf16[8192,512]{1,0:T(8,128)(2,1)} %bitcast.77, s32[512,256]{1,0:T(8,128)S(1)} %copy-done), kind=kOutput, calls=%fused_computation.7 | convolution fusion | flops 2149711872 | bytes 25690112 | tf_op jit(solution)/shard_map/dot_general | solution.py:76
  328.3 6.1 %convolution_add_fusion.4 = f32[8192,256]{1,0:T(8,128)S(1)} fusion(f32[8192,256]{1,0:T(8,128)S(1)} %convolution_add_fusion.5, bf16[8192,512]{1,0:T(8,128)(2,1)} %bitcast.76, s32[512,256]{1,0:T(8,128)S(1)} %copy-done), kind=kOutput, calls=%fused_computation.6 | convolution fusion | flops 2149711872 | bytes 25690112 | tf_op jit(solution)/shard_map/dot_general | solution.py:76
  336.9 6.2 %convolution_add_fusion.2 = f32[8192,256]{1,0:T(8,128)S(1)} fusion(f32[8192,256]{1,0:T(8,128)S(1)} %convolution_add_fusion.3, bf16[8192,512]{1,0:T(8,128)(2,1)} %bitcast.72, s32[512,256]{1,0:T(8,128)S(1)} %copy-done), kind=kOutput, calls=%fused_computation.4 | convolution fusion | flops 2149711872 | bytes 25690112 | tf_op jit(solution)/shard_map/dot_general | solution.py:76
  343.1 6.0 %convolution_add_fusion.1 = f32[8192,256]{1,0:T(8,128)S(1)} fusion(f32[8192,256]{1,0:T(8,128)S(1)} %convolution_add_fusion.2, bf16[8192,512]{1,0:T(8,128)(2,1)} %bitcast.71, s32[512,256]{1,0:T(8,128)S(1)} %copy-done), kind=kOutput, calls=%fused_computation.3 | convolution fusion | flops 2149711872 | bytes 25690112 | tf_op jit(solution)/shard_map/dot_general | solution.py:76
  349.1 9.2 %fusion = f32[8192,256]{1,0:T(8,128)} fusion(f32[8192,256]{1,0:T(8,128)S(1)} %convolution_add_fusion.1, bf16[8192,512]{1,0:T(8,128)(2,1)} %bitcast.70, s32[512,256]{1,0:T(8,128)S(1)} %copy-done), kind=kOutput, calls=%fused_computation.2 | convolution fusion | flops 2151809024 | bytes 25690112 | tf_op jit(solution)/shard_map/dot_general | solution.py:76
  358.3 39.2 %all-reduce.3.cloned.1.call-done = f32[8192,256]{1,0:T(8,128)} async-done(((f32[8192,256]{1,0:T(8,128)}), f32[8192,256]{1,0:T(8,128)}) %all-reduce.3.cloned.1.call-update) | async-done | bytes 8388624 | tf_op jit(solution)/shard_map/psum | solution.py:79
  397.5 3.8 fusion.17
  (39 shorter events, 11.6 us)
Async XLA Ops:
  7.6 69.2 %collective-permute-start = (bf16[511,512]{1,0:T(8,128)(2,1)S(1)}, bf16[511,512]{1,0:T(8,128)(2,1)S(1)}, u32[]{:S(2)}, u32[]{:S(2)}) collective-permute-start(bf16[511,512]{1,0:T(8,128)(2,1)S(1)} %slice.73), channel_id=1, source_target_pairs={{2,0},{4,2},{6,4},{8,6},{10,8},{12,10},{14,12},{3,1},{5,3},{7,5},{... | collective-permute-start | bytes 1569800 | tf_op jit(solution)/shard_map/ppermute | solution.py:19
  41.0 7.3 %copy-start.1 = (bf16[512,4606]{1,0:T(8,128)(2,1)S(1)}, bf16[512,4606]{1,0:T(8,128)(2,1)}, u32[]{:S(2)}) copy-start(bf16[512,4606]{1,0:T(8,128)(2,1)} %convert_element_type.50) | copy-start | bytes 14149636
  48.3 12.6 %slice-start.2 = ((s8[33546240]{0:T(1024)(128)(4,1)}), s8[4194304]{0:T(1024)(128)(4,1)S(1)}, s32[]{:S(2)}) async-start(s8[33546240]{0:T(1024)(128)(4,1)} %bitcast.81), calls=%async_computation.4 | async-start | bytes 8388608
  48.3 12.6 %slice-start.3 = ((s8[33546240]{0:T(1024)(128)(4,1)}), s8[4194304]{0:T(1024)(128)(4,1)S(1)}, s32[]{:S(2)}) async-start(s8[33546240]{0:T(1024)(128)(4,1)} %bitcast.81), calls=%async_computation.5 | async-start | bytes 8388608
  48.3 12.6 %slice-start.4 = ((s8[33546240]{0:T(1024)(128)(4,1)}), s8[4194304]{0:T(1024)(128)(4,1)S(1)}, s32[]{:S(2)}) async-start(s8[33546240]{0:T(1024)(128)(4,1)} %bitcast.81), calls=%async_computation.6 | async-start | bytes 8388608
  48.3 12.6 %slice-start.5 = ((s8[33546240]{0:T(1024)(128)(4,1)}), s8[4194304]{0:T(1024)(128)(4,1)S(1)}, s32[]{:S(2)}) async-start(s8[33546240]{0:T(1024)(128)(4,1)} %bitcast.81), calls=%async_computation.7 | async-start | bytes 8388608
  48.3 12.6 %slice-start.6 = ((s8[33546240]{0:T(1024)(128)(4,1)}), s8[4194304]{0:T(1024)(128)(4,1)S(1)}, s32[]{:S(2)}) async-start(s8[33546240]{0:T(1024)(128)(4,1)} %bitcast.81), calls=%async_computation.8 | async-start | bytes 8388608
  54.3 6.6 %slice-start.7 = ((s8[33546240]{0:T(1024)(128)(4,1)}), s8[4194304]{0:T(1024)(128)(4,1)S(1)}, s32[]{:S(2)}) async-start(s8[33546240]{0:T(1024)(128)(4,1)} %bitcast.81), calls=%async_computation.9 | async-start | bytes 8388608
  54.3 6.7 %slice-start.8 = ((s8[33546240]{0:T(1024)(128)(4,1)}), s8[4194304]{0:T(1024)(128)(4,1)S(1)}, s32[]{:S(2)}) async-start(s8[33546240]{0:T(1024)(128)(4,1)} %bitcast.81), calls=%async_computation.10 | async-start | bytes 8388608
  54.3 8.0 %slice-start.9 = ((s8[33546240]{0:T(1024)(128)(4,1)}), s8[4186112]{0:T(1024)(128)(4,1)S(1)}, s32[]{:S(2)}) async-start(s8[33546240]{0:T(1024)(128)(4,1)} %bitcast.81), calls=%async_computation.11 | async-start | bytes 8372224
  89.3 101.4 %all-to-all-start = ((bf16[8,512,512]{2,0,1:T(8,128)(2,1)}), bf16[8,512,512]{2,0,1:T(8,128)(2,1)}, u32[]{:S(2)}, u32[]{:S(2)}) async-start(bf16[8,512,512]{2,0,1:T(8,128)(2,1)} %copy.5), calls=%async_computation | async-start | bytes 8388608 | tf_op jit(solution)/shard_map/all_to_all | solution.py:58
  97.8 299.8 %all-reduce.3.cloned.1.call-start = ((), (), s32[]{:S(2)}) async-start(), calls=%async_computation.1 | async-start | bytes 16777216 | tf_op jit(solution)/shard_map/psum | solution.py:79
  226.6 10.9 %copy-start = (s32[512,256]{1,0:T(8,128)S(1)}, s32[512,256]{1,0:T(8,128)}, u32[]{:S(2)}) copy-start(s32[512,256]{1,0:T(8,128)} %param.5) | copy-start | bytes 1572868
  236.3 22.9 %collective-permute-start.1 = (bf16[2,64,7,512]{3,1,2,0:T(8,128)(2,1)S(1)}, bf16[2,64,7,512]{3,1,2,0:T(8,128)(2,1)S(1)}, u32[]{:S(2)}, u32[]{:S(2)}) collective-permute-start(bf16[2,64,7,512]{3,1,2,0:T(8,128)(2,1)S(1)} %copy.9), channel_id=1, source_target_pairs={{2,0},{4,2},{6,4},{8,6},{10,8},{12,10},{14,12},{3,1},{5,3},{7,5},{... | collective-permute-start | bytes 2752520 | tf_op jit(solution)/shard_map/ppermute | solution.py:19
  322.1 12.3 %slice-start = ((s8[8388608]{0:T(1024)(128)(4,1)}), s8[4194304]{0:T(1024)(128)(4,1)S(1)}, s32[]{:S(2)}) async-start(s8[8388608]{0:T(1024)(128)(4,1)} %bitcast.73), calls=%async_computation.2 | async-start | bytes 8388608
  328.3 6.2 %slice-start.1 = ((s8[8388608]{0:T(1024)(128)(4,1)}), s8[4194304]{0:T(1024)(128)(4,1)S(1)}, s32[]{:S(2)}) async-start(s8[8388608]{0:T(1024)(128)(4,1)} %bitcast.73), calls=%async_computation.3 | async-start | bytes 8388608
Sparse Core Ops, SparseCore 0:
  358.4 39.0 all-reduce.2
where the time goes:
time: 416 us; the launch traced here: 408 us
  waiting for transfers between devices  145 us (35%)
  local copies, waits for them, and re-layouts  135 us (32%)
  matrix products  99.4 us (24%)
  between operations  13.9 us (3%)
  starting transfers between devices  11.1 us (3%)
  other arithmetic  4.64 us (1%)
    all_to_all x1, waiting for transfers between devices, body(): lax.all_to_all(profiles, 'tm', split_axis=1, concat_axis=0, tiled=True)  92.8 us
    dot_general x8, matrix products, body(): jnp.dot(shifted_list[offset], selector, preferred_element_type=jnp.float32)  53.6 us
    slice x1, local copies, waits for them, and re-layouts, body(): spec_ext[:, :, offset:offset + delay_rows, :]  52.9 us
    dot_general x8, matrix products, body(): jnp.dot(toeplitz, segment, preferred_element_type=jnp.float32) * norm_code  40.2 us
    psum x1, waiting for transfers between devices, body(): summed = lax.psum(partial_sum * norm_hydro, 'hyd')  39.2 us
    unnamed x28, local copies, waits for them, and re-layouts  22.6 us
    another operation x2, local copies, waits for them, and re-layouts, toeplitz_code(): tiled = jnp.tile(padded, DELAYS)[:DELAYS * seg_len]  14.3 us
    another operation x1, local copies, waits for them, and re-layouts, body(): spec_ext[:, :, offset:offset + delay_rows, :]  13.6 us
  transfers between devices with their start and end apart: 4, of which 3 were waited for; matrix products, arithmetic and copies ran while one was open for 19% of the time, Pallas kernels for 0%

commit v1 on v0

v1 whole, which is shorter than its diff:
```python
import functools
import math

import jax
import jax.numpy as jnp
from jax import lax
from jax.experimental import pallas as pl
from jax.experimental.pallas import tpu as pltpu
from jax.sharding import PartitionSpec as P

CODE = 4095
HYDRO = 1024
DELAYS = 512
PERIODS = 64
BEAMS = 256
MAXLAG = 8

ROWS = 8
STEP = DELAYS // ROWS
OUT_ROWS = ROWS * (STEP + MAXLAG)
CODE_ROWS = OUT_ROWS + ROWS * 14
WIDTH = 4736
MAIN = 4096
EXTRA = WIDTH - MAIN
LATE = 528
MESH = pl.DeviceIdType.MESH


def build_code(base_ref, code_ref):
    def fill(pair, rolled):
        rolled_1 = pltpu.roll(rolled, 1, 1)
        rolled_2 = pltpu.roll(rolled_1, 1, 1)
        at = pl.ds(pl.multiple_of(pair * 16, 16), 16)
        code_ref[0, at, :] = jnp.concatenate([rolled, rolled_1], 0).astype(jnp.bfloat16)
        code_ref[1, at, :] = jnp.concatenate([rolled_1, rolled_2], 0).astype(jnp.bfloat16)
        return rolled_2

    lax.fori_loop(0, CODE_ROWS // 16, fill, base_ref[...])


def kernel(
    periods, peers, record, base, lags, head, rest, out,
    code, seg, sel, even, odd, own, half_out, half_in, ready, got, late,
    main_sem, extra_sem, half_send, half_recv, send_sem, recv_sem, late_send, late_recv,
):
    me = lax.axis_index("tm")
    hyd = lax.axis_index("hyd")
    delays = DELAYS // peers
    beams = BEAMS // 2
    width = record.shape[1]

    barrier = pltpu.get_barrier_semaphore()
    for step in range(1, peers):
        pl.semaphore_signal(
            barrier, inc=1, device_id={"tm": lax.rem(me + step, peers)}, device_id_type=MESH
        )
    pl.semaphore_signal(barrier, inc=1, device_id={"hyd": 1 - hyd}, device_id_type=MESH)

    def main_copy(period, slot):
        start = pl.multiple_of((period * CODE) // 16 * 16, 16)
        return pltpu.make_async_copy(
            record.at[pl.ds(start, MAIN)], seg.at[slot, pl.ds(0, MAIN)], main_sem.at[slot]
        )

    def extra_copy(period, slot):
        start = pl.multiple_of((period * CODE) // 16 * 16 + MAIN, 16)
        return pltpu.make_async_copy(
            record.at[pl.ds(start, EXTRA)], seg.at[slot, pl.ds(MAIN, EXTRA)], extra_sem.at[slot]
        )

    def late_copy():
        return pltpu.make_async_remote_copy(
            src_ref=head, dst_ref=late, send_sem=late_send, recv_sem=late_recv,
            device_id={"tm": lax.max(me - 1, 0)}, device_id_type=MESH,
        )

    def half_copy(period):
        return pltpu.make_async_remote_copy(
            src_ref=half_out.at[period], dst_ref=half_in.at[period],
            send_sem=half_send.at[period], recv_sem=half_recv.at[period],
            device_id={"hyd": 1 - hyd}, device_id_type=MESH,
        )

    def out_copy(period, peer):
        return pltpu.make_async_remote_copy(
            src_ref=ready.at[period, pl.ds(pl.multiple_of(peer * delays, 16), delays)],
            dst_ref=got.at[me * periods + period],
            send_sem=send_sem.at[peer, period], recv_sem=recv_sem.at[me, period],
            device_id={"tm": peer}, device_id_type=MESH,
        )

    def in_wait(period, peer):
        pltpu.make_async_remote_copy(
            src_ref=ready.at[period, pl.ds(0, delays)],
            dst_ref=got.at[peer * periods + period],
            send_sem=send_sem.at[peer, period], recv_sem=recv_sem.at[peer, period],
            device_id={"tm": peer}, device_id_type=MESH,
        ).wait_recv()

    main_copy(0, 0).start()
    extra_copy(0, 0).start()
    build_code(base, code)
    for offset in range(MAXLAG):
        sel[pl.ds(offset * width, width), :] = jnp.where(
            lags[...] == offset, 1.0, 0.0
        ).astype(jnp.bfloat16)

    pl.semaphore_wait(barrier, peers)

    @pl.when(me > 0)
    def _():
        late_copy().start()

    def pass_on(period):
        half_copy(period).wait_recv()
        total = own[...] + half_in[period].astype(jnp.float32)
        own[...] = total
        for j in range(ROWS):
            ready[period, pl.ds(j * STEP, STEP), :] = own[
                pl.ds(j, STEP, stride=ROWS), :
            ].astype(jnp.bfloat16)
        got[me * periods + period] = ready[
            period, pl.ds(pl.multiple_of(me * delays, 16), delays), :
        ]

        def send(step, carry):
            out_copy(period, lax.rem(me + step, peers)).start()
            return carry

        lax.fori_loop(1, peers, send, 0)

    def one_period(period, carry):
        slot = lax.rem(period, 2)
        main_copy(period, slot).wait()

        @pl.when(period < periods - 1)
        def _():
            extra_copy(period, slot).wait()
            main_copy(period + 1, 1 - slot).start()

        @pl.when(period < periods - 2)
        def _():
            extra_copy(period + 1, 1 - slot).start()

        @pl.when(period == periods - 1)
        def _():
            @pl.when(me < peers - 1)
            def _():
                late_copy().wait_recv()

            @pl.when(me == peers - 1)
            def _():
                late[...] = jnp.zeros_like(late)

            seg[slot, pl.ds(MAIN + 16, LATE - 16), :] = late[pl.ds(16, LATE - 16), :]
            seg[slot, pl.ds(MAIN, 16), :] = late[pl.ds(0, 16), :] + rest[...]
            seg[slot, pl.ds(MAIN + LATE, EXTRA - LATE), :] = jnp.zeros(
                (EXTRA - LATE, width), jnp.bfloat16
            )

        lead = lax.rem(period * CODE, 16)
        parity = lax.rem(lead, 2)
        first = pl.multiple_of((lead - parity) * ROWS, 16)
        profile = jnp.dot(
            code[parity, pl.ds(first, OUT_ROWS), :], seg[slot], preferred_element_type=jnp.float32
        ) * (1.0 / math.sqrt(CODE))
        row = lax.broadcasted_iota(jnp.int32, (ROWS * MAXLAG, width), 0)
        edge = jnp.where(row % ROWS == ROWS - 1, 0.0, profile[DELAYS:])
        profile = jnp.concatenate([profile[:DELAYS], edge], 0)
        even[...] = profile.astype(jnp.bfloat16)
        odd[...] = profile[ROWS : OUT_ROWS - ROWS].astype(jnp.bfloat16)
        shifted = []
        for offset in range(MAXLAG):
            source = odd if offset % 2 else even
            shifted.append(source[pl.ds(offset // 2 * 16, DELAYS), :])
        beam = jnp.dot(
            jnp.concatenate(shifted, 1), sel[...], preferred_element_type=jnp.float32
        ) * (1.0 / math.sqrt(HYDRO))

        @pl.when(period > 0)
        def _():
            pass_on(period - 1)

        first_half, second_half = beam[:, :beams], beam[:, beams:]
        own[...] = jnp.where(hyd == 0, first_half, second_half)
        half_out[period] = jnp.where(hyd == 0, second_half, first_half).astype(jnp.bfloat16)
        half_copy(period).start()
        return carry

    lax.fori_loop(0, periods, one_period, 0)
    pass_on(periods - 1)

    @pl.when(me > 0)
    def _():
        late_copy().wait_send()

    def finish(period, carry):
        half_copy(period).wait_send()

        def one(step, carry):
            peer = lax.rem(me + step, peers)
            in_wait(period, peer)
            out_copy(period, peer).wait_send()
            return carry

        return lax.fori_loop(1, peers, one, carry)

    lax.fori_loop(0, periods, finish, 0)
    out[...] = got[...]


def beam_sums(record, chips, steer_lags, peers):
    rows, width = record.shape
    periods = rows // CODE
    delays = DELAYS // peers
    beams = BEAMS // 2
    whole_rows = rows // 16 * 16
    over = rows - whole_rows
    code = chips.astype(jnp.float32)
    base = jnp.stack(
        [jnp.pad(code, (STEP * j, WIDTH - CODE - STEP * j)) for j in range(ROWS)]
    )
    head = jnp.pad(record[: DELAYS - 1], ((over, LATE - over - DELAYS + 1), (0, 0)))
    rest = jnp.pad(record[whole_rows:], ((0, 16 - over), (0, 0)))
    vmem = pl.BlockSpec(memory_space=pltpu.VMEM)
    dma = pltpu.SemaphoreType.DMA
    bf16, f32 = jnp.bfloat16, jnp.float32
    flops = 2 * periods * (OUT_ROWS * WIDTH * width + DELAYS * MAXLAG * width * BEAMS)
    return pl.pallas_call(
        functools.partial(kernel, periods, peers),
        out_shape=jax.ShapeDtypeStruct((PERIODS, delays, beams), bf16),
        in_specs=[pl.BlockSpec(memory_space=pl.ANY), vmem, vmem, vmem, vmem],
        out_specs=vmem,
        scratch_shapes=[
            pltpu.VMEM((2, CODE_ROWS, WIDTH), bf16),
            pltpu.VMEM((2, WIDTH, width), bf16),
            pltpu.VMEM((MAXLAG * width, BEAMS), bf16),
            pltpu.VMEM((OUT_ROWS, width), bf16),
            pltpu.VMEM((OUT_ROWS - 2 * ROWS, width), bf16),
            pltpu.VMEM((DELAYS, beams), f32),
            pltpu.VMEM((periods, DELAYS, beams), bf16),
            pltpu.VMEM((periods, DELAYS, beams), bf16),
            pltpu.VMEM((periods, DELAYS, beams), bf16),
            pltpu.VMEM((PERIODS, delays, beams), bf16),
            pltpu.VMEM((LATE, width), bf16),
            dma((2,)), dma((2,)), dma((periods,)), dma((periods,)),
            dma((peers, periods)), dma((peers, periods)), dma, dma,
        ],
        compiler_params=pltpu.CompilerParams(
            collective_id=0, has_side_effects=True, vmem_limit_bytes=60 * 1024 * 1024
        ),
        cost_estimate=pl.CostEstimate(
            flops=flops, bytes_accessed=2 * rows * width, transcendentals=0
        ),
    )(record, base, steer_lags, head, rest)


def power_kernel(delays, table, got, out, wide):
    wide[...] = got[...].astype(jnp.float32)
    group = 4
    for first in range(0, delays, group):
        columns = [
            wide[pl.ds(first + k, PERIODS, stride=delays), :].astype(jnp.bfloat16)
            for k in range(group)
        ]
        spectrum = jnp.dot(
            table[...], jnp.concatenate(columns, 1), preferred_element_type=jnp.float32
        )
        real, imag = spectrum[:PERIODS], spectrum[PERIODS:]
        power = real * real + imag * imag
        beams = power.shape[1] // group
        for k in range(group):
            out[pl.ds(first + k, PERIODS, stride=delays), :] = power[
                :, k * beams : (k + 1) * beams
            ]


def dft_table(length):
    freq = jnp.arange(length, dtype=jnp.int32)
    phase = (freq[:, None] * freq[None, :] % length).astype(jnp.float32) * (2.0 * math.pi / length)
    weight = 1.0 / math.sqrt(length)
    return jnp.concatenate([jnp.cos(phase) * weight, -jnp.sin(phase) * weight], 0).astype(
        jnp.bfloat16
    )


def body(record, chips, steer_lags):
    got = beam_sums(record, chips, steer_lags, lax.axis_size("tm"))
    periods, delays, beams = got.shape
    vmem = pl.BlockSpec(memory_space=pltpu.VMEM)
    power = pl.pallas_call(
        functools.partial(power_kernel, delays),
        out_shape=jax.ShapeDtypeStruct((periods * delays, beams), jnp.float32),
        in_specs=[vmem, vmem],
        out_specs=vmem,
        scratch_shapes=[pltpu.VMEM((periods * delays, beams), jnp.float32)],
        compiler_params=pltpu.CompilerParams(vmem_limit_bytes=32 * 1024 * 1024),
    )(dft_table(PERIODS), got.reshape(periods * delays, beams))
    return power.reshape(periods, delays, beams)


def solution(mesh):
    in_specs = (P(("runs", "tm"), "hyd"), P(), P("hyd", None))
    out_specs = P("runs", "tm", "hyd")
    return jax.shard_map(body, mesh=mesh, in_specs=in_specs, out_specs=out_specs, check_vma=False)
```

time: 416 us -> 85.9 us (0.21); the launches traced: 408 us -> 85.6 us
  waiting for transfers between devices: 145 us -> 0 us
  local copies, waits for them, and re-layouts: 135 us -> 5.5 us
  matrix products: 99.4 us -> 0 us
  Pallas kernels: 0 us -> 79.1 us
  between operations: 13.9 us -> 0.1 us
  starting transfers between devices: 11.1 us -> 0 us
    dot_general x17 -> x0, matrix products: 99.4 us -> none  [the longest x8 53.6 us: body(): jnp.dot(shifted_list[offset], selector, preferred_element_type=jnp.float32)]
    all_to_all x1 -> x0, waiting for transfers between devices: 92.8 us -> none  [body(): lax.all_to_all(profiles, 'tm', split_axis=1, concat_axis=0, tiled=True)]
    pallas_call x0 -> x2, Pallas kernels: none -> 79.1 us  [the longest x1 74.9 us: beam_sums(): pl.pallas_call(functools.partial(kernel, periods, peers), out_shape=jax.S...]
    slice x4 -> x2, local copies, waits for them, and re-layouts: 61 us -> 1.77 us  [the longest x1 1.08 us: beam_sums(): record[:DELAYS - 1]]
    psum x1 -> x0, waiting for transfers between devices: 39.2 us -> none  [body(): summed = lax.psum(partial_sum * norm_hydro, 'hyd')]
    another operation x5 -> x9, local copies, waits for them, and re-layouts: 34.6 us -> 0.99 us  [beam_sums(): jnp.stack([jnp.pad(code, (STEP * j, WIDTH - CODE - STEP * j)) for j in ra...]
    unnamed x28 -> x2, local copies, waits for them, and re-layouts: 22.6 us -> 1.22 us
    ppermute x2 -> x0, waiting for transfers between devices: 12.5 us -> none  [passed_along(): return lax.ppermute(array, axis, pairs)]
  transfers between devices with their start and end apart: 4 -> 0, of which waited for: 3 -> 0; matrix products, arithmetic and copies ran while one was open for 19% -> 0% of each run, Pallas kernels for 0% -> 0%
where the time goes in v1:
time: 85.9 us; the launch traced here: 85.6 us
  Pallas kernels  79.1 us (92%)
  local copies, waits for them, and re-layouts  5.5 us (6%)
  other arithmetic  0.88 us (1%)
    pallas_call x1, Pallas kernels, beam_sums(): pl.pallas_call(functools.partial(kernel, periods, peers), out_shape=jax.S...  74.9 us
    pallas_call x1, Pallas kernels, body(): pl.pallas_call(functools.partial(power_kernel, delays), out_shape=jax.Sha...  4.27 us

profile of v1, /device:TPU:0, one launch (start us, length us, event | category | flops | bytes accessed | tf_op | source)
XLA Modules:
  0.0 85.6 jit_solution(5446853487435172662)
XLA Ops:
  0.0 0.7 slice.7
  0.7 0.6 pad.49.rest
  1.3 0.7 convert_element_type.30
  2.0 0.2 multiply_convert_fusion
  2.2 0.1 fusion.6
  2.5 0.9 %stack.35.base = f32[8,4736]{1,0:T(8,128)} concatenate(f32[1,4736]{1,0:T(1,128)S(1)} %stack.27, f32[1,4736]{1,0:T(1,128)S(1)} %stack.28, f32[1,4736]{1,0:T(1,128)S(1)} %stack.29, f32[1,4736]{1,0:T(1,128)S(1)} %stack.30, f32[1,4736]{1,0:T(1,128)S(1)} %stack.31, f32[1,4736]{1,0:T(1,128)S(1)} %stack.32, f32[1,4736]{1,0:T(1,128)S(1)} %stack.33, f32[1,4736]{1,0:T(1,128)S(1)} %stack.34), dimensions={0} | concatenate | bytes 303104 | tf_op jit(solution)/shard_map/stack | solution.py:220
  3.3 1.1 %slice.6 = bf16[511,512]{1,0:T(8,128)(2,1)S(1)} slice(bf16[32760,512]{1,0:T(8,128)(2,1)} %record.1), slice={[0:511], [0:512]} | slice | bytes 1046528 | tf_op jit(solution)/shard_map/slice | solution.py:223
  4.4 0.8 pad.48.head
  5.3 74.9 %shard_map.37 = bf16[64,64,128]{2,1,0:T(8,128)(2,1)} custom-call(bf16[32760,512]{1,0:T(8,128)(2,1)} %record.1, f32[8,4736]{1,0:T(8,128)} %stack.35.base, s32[512,256]{1,0:T(8,128)} %lags.1, bf16[528,512]{1,0:T(8,128)(2,1)} %pad.48.head, bf16[16,512]{1,0:T(8,128)(2,1)} %pad.49.rest), custom_call_target="tpu_custom_call" | custom-call | flops 30937186304 | bytes 33546240 | tf_op jit(solution)/shard_map/pallas_call | solution.py:229
  80.1 0.0 copy-start
  80.1 1.2 %copy-done = bf16[64,64,128]{2,1,0:T(8,128)(2,1)S(1)} copy-done((bf16[64,64,128]{2,1,0:T(8,128)(2,1)S(1)}, bf16[64,64,128]{2,1,0:T(8,128)(2,1)}, u32[]{:S(2)}) %copy-start) | copy-done | bytes 1048600
  81.3 4.3 %shard_map.38 = f32[4096,128]{1,0:T(8,128)} custom-call(bf16[128,64]{1,0:T(8,128)(2,1)S(1)} %pad_maximum_fusion.table, bf16[4096,128]{1,0:T(8,128)(2,1)S(1)} %bitcast.2), custom_call_target="tpu_custom_call" | custom-call | tf_op jit(solution)/shard_map/pallas_call | solution.py:291
  (9 shorter events, 0.1 us)
Async XLA Ops:
  80.1 1.2 %copy-start = (bf16[64,64,128]{2,1,0:T(8,128)(2,1)S(1)}, bf16[64,64,128]{2,1,0:T(8,128)(2,1)}, u32[]{:S(2)}) copy-start(bf16[64,64,128]{2,1,0:T(8,128)(2,1)} %shard_map.37) | copy-start | bytes 3145732

commit v2 on v1

--- a/solution.py
+++ b/solution.py
@@ -18,6 +18,7 @@
 ROWS = 8
 STEP = DELAYS // ROWS
 OUT_ROWS = ROWS * (STEP + MAXLAG)
+PAIR_ROWS = DELAYS + 2 * ROWS
 CODE_ROWS = OUT_ROWS + ROWS * 14
 WIDTH = 4736
 MAIN = 4096
@@ -26,7 +27,7 @@
 MESH = pl.DeviceIdType.MESH
 
 
-def build_code(base_ref, code_ref):
+def build_code(chips_ref, code_ref):
     def fill(pair, rolled):
         rolled_1 = pltpu.roll(rolled, 1, 1)
         rolled_2 = pltpu.roll(rolled_1, 1, 1)
@@ -35,12 +36,17 @@
         code_ref[1, at, :] = jnp.concatenate([rolled_1, rolled_2], 0).astype(jnp.bfloat16)
         return rolled_2
 
-    lax.fori_loop(0, CODE_ROWS // 16, fill, base_ref[...])
+    chips = jnp.broadcast_to(chips_ref[...], (ROWS, WIDTH))
+    row = lax.broadcasted_iota(jnp.int32, (ROWS, WIDTH), 0)
+    base = chips
+    for j in range(1, ROWS):
+        base = jnp.where(row == j, pltpu.roll(chips, STEP * j, 1), base)
+    lax.fori_loop(0, CODE_ROWS // 16, fill, base)
 
 
 def kernel(
-    periods, peers, record, base, lags, head, rest, out,
-    code, seg, sel, even, odd, own, half_out, half_in, ready, got, late,
+    periods, peers, record, chip_row, lags, rest, out,
+    code, seg, sel, even, own, half_out, half_in, ready, got, late,
     main_sem, extra_sem, half_send, half_recv, send_sem, recv_sem, late_send, late_recv,
 ):
     me = lax.axis_index("tm")
@@ -70,7 +76,7 @@
 
     def late_copy():
         return pltpu.make_async_remote_copy(
-            src_ref=head, dst_ref=late, send_sem=late_send, recv_sem=late_recv,
+            src_ref=record.at[pl.ds(0, DELAYS)], dst_ref=late, send_sem=late_send, recv_sem=late_recv,
             device_id={"tm": lax.max(me - 1, 0)}, device_id_type=MESH,
         )
 
@@ -99,9 +105,9 @@
 
     main_copy(0, 0).start()
     extra_copy(0, 0).start()
-    build_code(base, code)
+    build_code(chip_row, code)
     for offset in range(MAXLAG):
-        sel[pl.ds(offset * width, width), :] = jnp.where(
+        sel[pl.ds(offset // 2 * width, width), pl.ds(offset % 2 * BEAMS, BEAMS)] = jnp.where(
             lags[...] == offset, 1.0, 0.0
         ).astype(jnp.bfloat16)
 
@@ -152,8 +158,15 @@
             def _():
                 late[...] = jnp.zeros_like(late)
 
-            seg[slot, pl.ds(MAIN + 16, LATE - 16), :] = late[pl.ds(16, LATE - 16), :]
-            seg[slot, pl.ds(MAIN, 16), :] = late[pl.ds(0, 16), :] + rest[...]
+            over = record.shape[0] % 16
+            seg[slot, pl.ds(MAIN, LATE), :] = jnp.concatenate(
+                [
+                    rest[...].astype(jnp.float32)[16 - over :],
+                    late[...].astype(jnp.float32),
+                    jnp.zeros((16 - over, width), jnp.float32),
+                ],
+                0,
+            ).astype(jnp.bfloat16)
             seg[slot, pl.ds(MAIN + LATE, EXTRA - LATE), :] = jnp.zeros(
                 (EXTRA - LATE, width), jnp.bfloat16
             )
@@ -168,19 +181,18 @@
         edge = jnp.where(row % ROWS == ROWS - 1, 0.0, profile[DELAYS:])
         profile = jnp.concatenate([profile[:DELAYS], edge], 0)
         even[...] = profile.astype(jnp.bfloat16)
-        odd[...] = profile[ROWS : OUT_ROWS - ROWS].astype(jnp.bfloat16)
-        shifted = []
-        for offset in range(MAXLAG):
-            source = odd if offset % 2 else even
-            shifted.append(source[pl.ds(offset // 2 * 16, DELAYS), :])
-        beam = jnp.dot(
-            jnp.concatenate(shifted, 1), sel[...], preferred_element_type=jnp.float32
-        ) * (1.0 / math.sqrt(HYDRO))
 
         @pl.when(period > 0)
         def _():
             pass_on(period - 1)
 
+        shifted = [even[pl.ds(pair * 16, PAIR_ROWS), :] for pair in range(MAXLAG // 2)]
+        pairs = jnp.dot(
+            jnp.concatenate(shifted, 1), sel[...], preferred_element_type=jnp.float32
+        )
+        beam = (pairs[:DELAYS, :BEAMS] + pairs[ROWS : ROWS + DELAYS, BEAMS:]) * (
+            1.0 / math.sqrt(HYDRO)
+        )
         first_half, second_half = beam[:, :beams], beam[:, beams:]
         own[...] = jnp.where(hyd == 0, first_half, second_half)
         half_out[period] = jnp.where(hyd == 0, second_half, first_half).astype(jnp.bfloat16)
@@ -214,14 +226,8 @@
     periods = rows // CODE
     delays = DELAYS // peers
     beams = BEAMS // 2
-    whole_rows = rows // 16 * 16
-    over = rows - whole_rows
-    code = chips.astype(jnp.float32)
-    base = jnp.stack(
-        [jnp.pad(code, (STEP * j, WIDTH - CODE - STEP * j)) for j in range(ROWS)]
-    )
-    head = jnp.pad(record[: DELAYS - 1], ((over, LATE - over - DELAYS + 1), (0, 0)))
-    rest = jnp.pad(record[whole_rows:], ((0, 16 - over), (0, 0)))
+    chip_row = jnp.pad(chips.astype(jnp.float32), (0, WIDTH - CODE))[None]
+    rest = record[rows - 16 :]
     vmem = pl.BlockSpec(memory_space=pltpu.VMEM)
     dma = pltpu.SemaphoreType.DMA
     bf16, f32 = jnp.bfloat16, jnp.float32
@@ -229,20 +235,19 @@
     return pl.pallas_call(
         functools.partial(kernel, periods, peers),
         out_shape=jax.ShapeDtypeStruct((PERIODS, delays, beams), bf16),
-        in_specs=[pl.BlockSpec(memory_space=pl.ANY), vmem, vmem, vmem, vmem],
+        in_specs=[pl.BlockSpec(memory_space=pl.ANY), vmem, vmem, vmem],
         out_specs=vmem,
         scratch_shapes=[
             pltpu.VMEM((2, CODE_ROWS, WIDTH), bf16),
             pltpu.VMEM((2, WIDTH, width), bf16),
-            pltpu.VMEM((MAXLAG * width, BEAMS), bf16),
+            pltpu.VMEM((MAXLAG // 2 * width, 2 * BEAMS), bf16),
             pltpu.VMEM((OUT_ROWS, width), bf16),
-            pltpu.VMEM((OUT_ROWS - 2 * ROWS, width), bf16),
             pltpu.VMEM((DELAYS, beams), f32),
             pltpu.VMEM((periods, DELAYS, beams), bf16),
             pltpu.VMEM((periods, DELAYS, beams), bf16),
             pltpu.VMEM((periods, DELAYS, beams), bf16),
             pltpu.VMEM((PERIODS, delays, beams), bf16),
-            pltpu.VMEM((LATE, width), bf16),
+            pltpu.VMEM((DELAYS, width), bf16),
             dma((2,)), dma((2,)), dma((periods,)), dma((periods,)),
             dma((peers, periods)), dma((peers, periods)), dma, dma,
         ],
@@ -252,7 +257,7 @@
         cost_estimate=pl.CostEstimate(
             flops=flops, bytes_accessed=2 * rows * width, transcendentals=0
         ),
-    )(record, base, steer_lags, head, rest)
+    )(record, chip_row, steer_lags, rest)
 
 
 def power_kernel(delays, table, got, out, wide):

time: 85.9 us -> 66.7 us (0.78)
  Pallas kernels: 79.1 us -> 62.3 us
  local copies, waits for them, and re-layouts: 5.5 us -> 3.16 us
    pallas_call x1, Pallas kernels: 74.9 us -> 58.1 us  [beam_sums(): pl.pallas_call(functools.partial(kernel, periods, peers), out_shape=jax.S...]
    pad x3 -> x1, local copies, waits for them, and re-layouts: 1.53 us -> 0.01 us  [beam_sums(): chip_row = jnp.pad(chips.astype(jnp.float32), (0, WIDTH - CODE))[None]]
    another operation x9 -> x0, local copies, waits for them, and re-layouts: 0.99 us -> none  [beam_sums(): jnp.stack([jnp.pad(code, (STEP * j, WIDTH - CODE - STEP * j)) for j in ra...]
    slice x2 -> x1, local copies, waits for them, and re-layouts: 1.77 us -> 1.32 us  [beam_sums(): rest = record[rows - 16:]]
where the time goes in v2:
time: 66.7 us; the launch traced here: 66.4 us
  Pallas kernels  62.3 us (93%)
  local copies, waits for them, and re-layouts  3.16 us (5%)
  other arithmetic  0.88 us (1%)
    pallas_call x1, Pallas kernels, beam_sums(): pl.pallas_call(functools.partial(kernel, periods, peers), out_shape=jax.S...  58.1 us
    pallas_call x1, Pallas kernels, body(): pl.pallas_call(functools.partial(power_kernel, delays), out_shape=jax.Sha...  4.22 us

profile of v2, /device:TPU:0, one launch (start us, length us, event | category | flops | bytes accessed | tf_op | source)
XLA Modules:
  0.0 66.4 jit_solution(8610382918727805149)
XLA Ops:
  0.0 0.7 %convert_element_type.12 = f32[4095]{0:T(1024)S(1)} convert(s32[4095]{0:T(1024)} %param.4) | non-fusion elementwise | flops 4095 | bytes 32760 | tf_op jit(solution)/shard_map/convert_element_type | solution.py:229
  0.7 0.6 broadcast_in_dim.2.chip_row
  1.3 1.3 %slice.3.rest = bf16[16,512]{1,0:T(8,128)(2,1)} slice(bf16[32760,512]{1,0:T(8,128)(2,1)} %record.1), slice={[32744:32760], [0:512]} | slice | bytes 32768 | tf_op jit(solution)/shard_map/slice | solution.py:230
  2.7 0.2 multiply_convert_fusion
  2.8 58.1 %shard_map.37 = bf16[64,64,128]{2,1,0:T(8,128)(2,1)} custom-call(bf16[32760,512]{1,0:T(8,128)(2,1)} %record.1, f32[1,4736]{1,0:T(1,128)} %broadcast_in_dim.2.chip_row, s32[512,256]{1,0:T(8,128)} %lags.1, bf16[16,512]{1,0:T(8,128)(2,1)} %slice.3.rest), custom_call_target="tpu_custom_call" | custom-call | flops 30937186304 | bytes 33546240 | tf_op jit(solution)/shard_map/pallas_call | solution.py:235
  60.9 0.0 copy-start
  60.9 1.2 %copy-done = bf16[64,64,128]{2,1,0:T(8,128)(2,1)S(1)} copy-done((bf16[64,64,128]{2,1,0:T(8,128)(2,1)S(1)}, bf16[64,64,128]{2,1,0:T(8,128)(2,1)}, u32[]{:S(2)}) %copy-start) | copy-done | bytes 1048600
  62.1 4.2 %shard_map.38 = f32[4096,128]{1,0:T(8,128)} custom-call(bf16[128,64]{1,0:T(8,128)(2,1)S(1)} %pad_maximum_fusion.table, bf16[4096,128]{1,0:T(8,128)(2,1)S(1)} %bitcast.2), custom_call_target="tpu_custom_call" | custom-call | tf_op jit(solution)/shard_map/pallas_call | solution.py:296
  (2 shorter events, 0.0 us)
Async XLA Ops:
  60.9 1.2 %copy-start = (bf16[64,64,128]{2,1,0:T(8,128)(2,1)S(1)}, bf16[64,64,128]{2,1,0:T(8,128)(2,1)}, u32[]{:S(2)}) copy-start(bf16[64,64,128]{2,1,0:T(8,128)(2,1)} %shard_map.37) | copy-start | bytes 3145732

commit v3 on v2

--- a/solution.py
+++ b/solution.py
@@ -30,7 +30,7 @@
 def build_code(chips_ref, code_ref):
     def fill(pair, rolled):
         rolled_1 = pltpu.roll(rolled, 1, 1)
-        rolled_2 = pltpu.roll(rolled_1, 1, 1)
+        rolled_2 = pltpu.roll(rolled, 2, 1)
         at = pl.ds(pl.multiple_of(pair * 16, 16), 16)
         code_ref[0, at, :] = jnp.concatenate([rolled, rolled_1], 0).astype(jnp.bfloat16)
         code_ref[1, at, :] = jnp.concatenate([rolled_1, rolled_2], 0).astype(jnp.bfloat16)

time: 66.7 us -> 63 us (0.945)
  Pallas kernels: 62.3 us -> 58.6 us
    pallas_call x1, Pallas kernels: 58.1 us -> 54.4 us  [beam_sums(): pl.pallas_call(functools.partial(kernel, periods, peers), out_shape=jax.S...]
where the time goes in v3:
time: 63 us; the launch traced here: 62.7 us
  Pallas kernels  58.6 us (93%)
  local copies, waits for them, and re-layouts  3.16 us (5%)
  other arithmetic  0.88 us (1%)
    pallas_call x1, Pallas kernels, beam_sums(): pl.pallas_call(functools.partial(kernel, periods, peers), out_shape=jax.S...  54.4 us
    pallas_call x1, Pallas kernels, body(): pl.pallas_call(functools.partial(power_kernel, delays), out_shape=jax.Sha...  4.22 us
    slice x1, local copies, waits for them, and re-layouts, beam_sums(): rest = record[rows - 16:]  1.32 us

profile of v3, /device:TPU:0, one launch (start us, length us, event | category | flops | bytes accessed | tf_op | source)
XLA Modules:
  0.0 62.7 jit_solution(8931752941721461261)
XLA Ops:
  0.0 0.7 %convert_element_type.12 = f32[4095]{0:T(1024)S(1)} convert(s32[4095]{0:T(1024)} %param.4) | non-fusion elementwise | flops 4095 | bytes 32760 | tf_op jit(solution)/shard_map/convert_element_type | solution.py:229
  0.7 0.6 broadcast_in_dim.2.chip_row
  1.3 1.3 %slice.3.rest = bf16[16,512]{1,0:T(8,128)(2,1)} slice(bf16[32760,512]{1,0:T(8,128)(2,1)} %record.1), slice={[32744:32760], [0:512]} | slice | bytes 32768 | tf_op jit(solution)/shard_map/slice | solution.py:230
  2.7 0.2 multiply_convert_fusion
  2.8 54.4 %shard_map.37 = bf16[64,64,128]{2,1,0:T(8,128)(2,1)} custom-call(bf16[32760,512]{1,0:T(8,128)(2,1)} %record.1, f32[1,4736]{1,0:T(1,128)} %broadcast_in_dim.2.chip_row, s32[512,256]{1,0:T(8,128)} %lags.1, bf16[16,512]{1,0:T(8,128)(2,1)} %slice.3.rest), custom_call_target="tpu_custom_call" | custom-call | flops 30937186304 | bytes 33546240 | tf_op jit(solution)/shard_map/pallas_call | solution.py:235
  57.2 0.0 copy-start
  57.2 1.2 %copy-done = bf16[64,64,128]{2,1,0:T(8,128)(2,1)S(1)} copy-done((bf16[64,64,128]{2,1,0:T(8,128)(2,1)S(1)}, bf16[64,64,128]{2,1,0:T(8,128)(2,1)}, u32[]{:S(2)}) %copy-start) | copy-done | bytes 1048600
  58.4 4.2 %shard_map.38 = f32[4096,128]{1,0:T(8,128)} custom-call(bf16[128,64]{1,0:T(8,128)(2,1)S(1)} %pad_maximum_fusion.table, bf16[4096,128]{1,0:T(8,128)(2,1)S(1)} %bitcast.2), custom_call_target="tpu_custom_call" | custom-call | tf_op jit(solution)/shard_map/pallas_call | solution.py:296
  (2 shorter events, 0.0 us)
Async XLA Ops:
  57.2 1.2 %copy-start = (bf16[64,64,128]{2,1,0:T(8,128)(2,1)S(1)}, bf16[64,64,128]{2,1,0:T(8,128)(2,1)}, u32[]{:S(2)}) copy-start(bf16[64,64,128]{2,1,0:T(8,128)(2,1)} %shard_map.37) | copy-start | bytes 3145732
